TPU v7x, 1024 devices: a whole 4x8x16 slice. The times are simulated.
1024 devices in a mesh: dp: 128 (over z, y), space: 8 (over x, core).
Axes of the slice: x: 4, y: 8, z: 16, core: 2. Of those that a mesh axis runs over, the one named last changes fastest.
Arguments:
- section_three: bfloat16 [128, 32, 32, 768], P('dp', 'space'), may hold values from -6 to 6
- dw_kernel: float32 [7, 7, 768], replicated, may hold values from -0.875 to 0.875
- dw_bias: float32 [768], replicated, may hold values from -3 to 3
- mix_gain: float32 [768], replicated, may hold values from 0.1 to 1.9
- w_expand: bfloat16 [768, 1536], replicated, may hold values from -0.21875 to 0.21875
- w_reduce: bfloat16 [1536, 768], replicated, may hold values from -0.15625 to 0.15625
- layer_scale: float32 [768], replicated, may hold values from 0.3 to 1.5
- down_gain: float32 [768], replicated, may hold values from 0.1 to 1.9
- w_down: bfloat16 [3072, 1536], P(None, 'space'), may hold values from -0.109375 to 0.109375
- owner_table: int32 [128, 256, 1], P('dp'), may hold values from 0 to 127; in each aligned block of 256 rows (0 to 255, 256 to 511, ..., all dimensions but the last counted through in order) at most 2 rows name the same one
- grad_packed: bfloat16 [128, 256, 1536], P('dp', None, 'space'), may hold values from -6 to 6
Outputs:
- packed_tokens: bfloat16 [128, 256, 1536], P('dp', None, 'space')
- grad_mixed: bfloat16 [128, 32, 32, 768], P('dp', 'space')
Inputs may be any that keep to these rules, and one draw needn't show every extreme that they name: `owner_table`: among the 256 tokens of one screenshot no owner is named more than 2 times, a bound that some block reaches.
All inputs are finite; a program needn't handle non-finite values.
Results may differ from a plain program's by a relative error of at most 0.018.
Values may be sent and summed in bfloat16 or wider, within the bound.
A program may use at most 32 MiB of HBM per device.

v0:
```python
import jax
import jax.numpy as jnp
from jax import lax
from jax.sharding import PartitionSpec as P

KS = 7


def padded_2(cells, sides, width):
    for axis, dim in sides:
        count = lax.axis_size(axis)
        ends = count - 1
        head = lax.slice_in_dim(cells, 0, width, axis=dim)
        tail = lax.slice_in_dim(cells, cells.shape[dim] - width, cells.shape[dim], axis=dim)
        cells = jnp.concatenate(
            [
                lax.ppermute(tail, axis, [(i, (i + 1) % count) for i in range(ends)]),
                cells,
                lax.ppermute(head, axis, [((i + 1) % count, i) for i in range(ends)]),
            ],
            axis=dim,
        )
    return cells


def depthwise(padded, kernel, height, width):
    total = jnp.zeros((height, width, kernel.shape[2]), jnp.float32)
    for offset_y in range(KS):
        for offset_x in range(KS):
            total = (
                total
                + padded[offset_y : offset_y + height, offset_x : offset_x + width]
                * kernel[offset_y, offset_x]
            )
    return total


def layer_norm(values):
    center = values - jnp.mean(values, axis=-1, keepdims=True)
    inv_std = lax.rsqrt(jnp.mean(center * center, axis=-1, keepdims=True) + 1e-06)
    return (center * inv_std, inv_std)


def norm_back(grad, normed, inv_std, gain):
    scaled = grad * gain
    return inv_std * (
        scaled
        - jnp.mean(scaled, axis=-1, keepdims=True)
        - normed * jnp.mean(scaled * normed, axis=-1, keepdims=True)
    )


def gelu_slope(pre):
    cumulative = 0.5 * (1.0 + lax.erf(pre * 0.7071067811865476))
    density = jnp.exp(-0.5 * pre * pre) * 0.3989422804014327
    return cumulative + pre * density


def to_patches(grid):
    height, width, channels = grid.shape
    return (
        grid.reshape(height // 2, 2, width // 2, 2, channels)
        .transpose(0, 2, 1, 3, 4)
        .reshape(height // 2 * (width // 2), 4 * channels)
    )


def from_patches(flat, height, width, channels):
    return (
        flat.reshape(height // 2, width // 2, 2, 2, channels)
        .transpose(0, 2, 1, 3, 4)
        .reshape(height, width, channels)
    )


def slot_index(targets, owners_count, capacity):
    onehot = (targets[:, None] == jnp.arange(owners_count, dtype=jnp.int32)[None, :]).astype(
        jnp.int32
    )
    earlier = jnp.cumsum(onehot, axis=0) - onehot
    ranking = jnp.sum(earlier * onehot, axis=1)
    return targets * capacity + ranking


def on_device(
    section_three,
    dw_kernel,
    dw_bias,
    mix_gain,
    w_expand,
    w_reduce,
    layer_scale,
    down_gain,
    w_down,
    owner_table,
    grad_packed,
):
    owners_count = lax.axis_size("dp")
    slot_count = grad_packed.shape[1]
    capacity = slot_count // owners_count
    band_height = section_three.shape[1]
    band_width = section_three.shape[2]
    channels = section_three.shape[3]
    half = KS // 2
    extended = padded_2(section_three, (("space", 1),), half)
    padded = jnp.pad(extended[0].astype(jnp.float32), ((0, 0), (half, half), (0, 0)))
    mixed = (depthwise(padded, dw_kernel, band_height, band_width) + dw_bias).reshape(
        band_height * band_width, channels
    )
    normed_one, inv_one = layer_norm(mixed)
    first = (normed_one * mix_gain).astype(jnp.bfloat16)
    pre = jnp.dot(first, w_expand, preferred_element_type=jnp.float32)
    hidden = jax.nn.gelu(pre, approximate=False).astype(jnp.bfloat16)
    residual = section_three[0].astype(jnp.float32).reshape(band_height * band_width, channels)
    block_out = residual + layer_scale * jnp.dot(
        hidden, w_reduce, preferred_element_type=jnp.float32
    )
    normed_two, inv_two = layer_norm(block_out)
    second = (normed_two * down_gain).astype(jnp.bfloat16)
    patches = to_patches(second.reshape(band_height, band_width, channels))
    tokens = jnp.dot(
        lax.all_gather(patches, "space", axis=0, tiled=True),
        w_down,
        preferred_element_type=jnp.float32,
    ).astype(jnp.bfloat16)
    targets = owner_table[0, :, 0]
    send_pos = slot_index(targets, owners_count, capacity)
    send_buffer = jnp.zeros((slot_count, tokens.shape[1]), jnp.bfloat16).at[send_pos].set(tokens)
    arrived = lax.all_to_all(send_buffer, "dp", split_axis=0, concat_axis=0, tiled=True)
    returned = lax.all_to_all(grad_packed[0], "dp", split_axis=0, concat_axis=0, tiled=True)
    grad_tokens = returned[send_pos]
    grad_patches = lax.psum_scatter(
        lax.dot_general(
            grad_tokens, w_down, (((1,), (1,)), ((), ())), preferred_element_type=jnp.float32
        ).astype(jnp.bfloat16),
        "space",
        scatter_dimension=0,
        tiled=True,
    ).astype(jnp.float32)
    grad_second = from_patches(grad_patches, band_height, band_width, channels).reshape(
        band_height * band_width, channels
    )
    grad_block = norm_back(grad_second, normed_two, inv_two, down_gain)
    grad_scaled = (grad_block * layer_scale).astype(jnp.bfloat16)
    grad_hidden = lax.dot_general(
        grad_scaled, w_reduce, (((1,), (1,)), ((), ())), preferred_element_type=jnp.float32
    )
    grad_pre = (grad_hidden * gelu_slope(pre)).astype(jnp.bfloat16)
    grad_first = lax.dot_general(
        grad_pre, w_expand, (((1,), (1,)), ((), ())), preferred_element_type=jnp.float32
    )
    grad_mixed = norm_back(grad_first, normed_one, inv_one, mix_gain).astype(jnp.bfloat16)
    return (arrived[None], grad_mixed.reshape(1, band_height, band_width, channels))


def solution(mesh):
    in_specs = (
        P("dp", "space", None, None),
        P(),
        P(),
        P(),
        P(),
        P(),
        P(),
        P(),
        P(None, "space"),
        P("dp", None, None),
        P("dp", None, "space"),
    )
    out_specs = (P("dp", None, "space"), P("dp", "space", None, None))
    return jax.shard_map(
        on_device, mesh=mesh, in_specs=in_specs, out_specs=out_specs, check_vma=False
    )
```

profile of v0, /device:TPU:1, one launch (start us, length us, event | category | flops | bytes accessed | tf_op | source)
XLA Modules:
  0.0 191.1 jit_solution(13166705747962115135)
XLA Ops:
  9.1 26.8 %all-to-all-start.1 = ((bf16[128,2,192]{2,1,0:T(2,128)(2,1)}), bf16[128,2,192]{2,1,0:T(2,128)(2,1)S(1)}, u32[]{:S(2)}, u32[]{:S(2)}) async-start(bf16[128,2,192]{2,1,0:T(2,128)(2,1)} %all_to_all.16), calls=%async_computation.1 | async-start | bytes 262144 | tf_op jit(solution)/shard_map/all_to_all | solution.py:130
  36.9 4.0 %collective-permute-start = (bf16[1,3,32,768]{3,2,1,0:T(8,128)(2,1)S(1)}, bf16[1,3,32,768]{3,2,1,0:T(8,128)(2,1)S(1)}, u32[]{:S(2)}, u32[]{:S(2)}) collective-permute-start(bf16[1,3,32,768]{3,2,1,0:T(8,128)(2,1)S(1)} %get-tuple-element.61), channel_id=1, source_target_pairs={{0,1},{1,2},{2,3},{3,4},{4,5},{5,6},{6,7},{8,9},{9,10},{10,11},{11... | collective-permute-start | bytes 442376 | tf_op jit(solution)/shard_map/ppermute | solution.py:17
  40.9 1.9 %collective-permute-start.1 = (bf16[1,3,32,768]{3,2,1,0:T(8,128)(2,1)S(1)}, bf16[1,3,32,768]{3,2,1,0:T(8,128)(2,1)S(1)}, u32[]{:S(2)}, u32[]{:S(2)}) collective-permute-start(bf16[1,3,32,768]{3,2,1,0:T(8,128)(2,1)S(1)} %get-tuple-element.62), channel_id=1, source_target_pairs={{1,0},{2,1},{3,2},{4,3},{5,4},{6,5},{7,6},{9,8},{10,9},{11,10},{12... | collective-permute-start | bytes 442376 | tf_op jit(solution)/shard_map/ppermute | solution.py:19
  45.5 1.4 slice_reduce_fusion.48
  46.9 2.1 %slice_reduce_fusion.47 = (f32[768]{0:T(1024)S(1)}, f32[768]{0:T(1024)}, f32[768]{0:T(1024)}, f32[768]{0:T(1024)}, f32[768]{0:T(1024)}, /*index=5*/f32[768]{0:T(...) fusion(f32[7,7,768]{2,1,0:T(8,128)} %param.12), kind=kLoop, calls=%fused_computation.302 | loop fusion | bytes 116736 | tf_op jit(solution)/shard_map/slice | solution.py:33
  49.0 2.4 %all-to-all-done.1 = bf16[128,2,192]{2,1,0:T(2,128)(2,1)S(1)} async-done(((bf16[128,2,192]{2,1,0:T(2,128)(2,1)}), bf16[128,2,192]{2,1,0:T(2,128)(2,1)S(1)}, u32[]{:S(2)}, u32[]{:S(2)}) %all-to-all-start.1) | async-done | bytes 98336 | tf_op jit(solution)/shard_map/all_to_all | solution.py:130
  51.5 1.2 gather_fusion
  52.7 3.0 %convolution_convert_fusion = bf16[256,3072]{1,0:T(8,128)(2,1)} fusion(bf16[256,192]{1,0:T(8,128)(2,1)S(1)} %gather_fusion, bf16[3072,192]{0,1:T(8,128)(2,1)} %param.19), kind=kOutput, calls=%fused_computation.2 | convolution fusion | flops 302776320 | bytes 2850816 | tf_op jit(solution)/shard_map/dot_general | solution.py:133
  57.3 5.3 %fusion.214 = (f32[4,32]{1,0:T(4,128)S(1)}, f32[4,32,768]{2,1,0:T(8,128)S(1)}) fusion(f32[768]{0:T(1024)} %param.13, f32[768]{0:T(1024)S(1)} %get-tuple-element.53, f32[768]{0:T(1024)S(1)} %get-tuple-element.54, f32[768]{0:T(1024)S(1)} %get-tuple-element.7, f32[768]{0:T(1024)S(1)} %get-tuple-element.8, f32[1,10,32,768]{3,2,1,0:T(8,128)S(1)} %get-tuple-element.58, ...), kind=kLoop, calls=%fused_computation.350 | loop fusion | flops 9731968 | bytes 4282880 | tf_op jit(solution)/shard_map/reduce_sum | solution.py:39
  63.7 1.2 copy-done.10
  64.9 2.1 %fusion.217 = (f32[128]{0:T(128)S(1)}, f32[128,768]{1,0:T(8,128)S(1)}) fusion(bf16[1536,768]{1,0:T(8,128)(2,1)S(1)} %copy-done.10, f32[128,1536]{1,0:T(8,128)S(1)} %fusion.218, f32[768]{0:T(1024)S(1)} %copy-done.11, bf16[128,768]{1,0:T(8,128)(2,1)S(1)} %bitcast.120), kind=kOutput, calls=%fused_computation.352 | convolution fusion | flops 315162496 | bytes 3739136 | tf_op jit(solution)/shard_map/dot_general | solution.py:115
  67.8 28.8 %reduce-scatter.2.cloned.1.call-done = bf16[32,3072]{1,0:T(8,128)(2,1)} async-done(((bf16[256,3072]{1,0:T(8,128)(2,1)}), bf16[32,3072]{1,0:T(8,128)(2,1)}) %reduce-scatter.2.cloned.1.call-update) | async-done | bytes 196624 | tf_op jit(solution)/shard_map/reduce_scatter | solution.py:132
  96.6 1.3 reshape.160
  98.7 2.0 %reshape_reshape.7 = f32[128,768]{1,0:T(8,128)} reshape(f32[2,2,16,2,768]{4,3,2,1,0:T(2,128)} %bitcast.119) | data formatting | bytes 786432 | tf_op jit(solution)/shard_map/reshape;reshape | solution.py:140
  100.7 2.3 %multiply_reduce_fusion.1 = (f32[128]{0:T(128)}, bf16[128,768]{1,0:T(8,128)(2,1)}) fusion(f32[128,768]{1,0:T(8,128)} %reshape_reshape.7, f32[128,768]{1,0:T(8,128)S(1)} %get-tuple-element.64, f32[768]{0:T(1024)S(1)} %copy-done.3, f32[128]{0:T(128)} %add_rsqrt_fusion.1, f32[128]{0:T(128)} %copy-done.7), kind=kLoop, calls=%fused_computation.194 | loop fusion | flops 688000 | bytes 987648 | tf_op jit(solution)/shard_map/reduce_sum | solution.py:49
  103.0 1.7 reshape_reshape.6
  104.7 1.7 copy.28
  106.4 1.7 reshape.156
  110.2 4.3 %fusion.213 = (f32[128]{0:T(128)}, f32[128]{0:T(128)}, f32[128,768]{1,0:T(8,128)S(1)}) fusion(f32[128]{0:T(128)S(1)} %rsqrt.20, f32[128]{0:T(128)S(1)} %div.29, f32[4,32,768]{2,1,0:T(8,128)S(1)} %get-tuple-element.56, f32[768]{0:T(1024)S(1)} %copy-done.5, bf16[768,1536]{1,0:T(8,128)(2,1)S(1)} %copy-done, bf16[1536,768]{1,0:T(8,128)(2,1)} %param.16, ...), kind=kOutput, calls=%fused_computation.349 | convolution fusion | flops 607420160 | bytes 7091200 | tf_op jit(solution)/shard_map/dot_general | solution.py:149
  114.5 28.6 %all-gather.2.cloned.1.call-done = bf16[256,3072]{1,0:T(8,128)(2,1)} async-done(((bf16[32,3072]{1,0:T(8,128)(2,1)}), bf16[256,3072]{1,0:T(8,128)(2,1)}) %all-gather.2.cloned.1.call-update) | async-done | bytes 1572880 | tf_op jit(solution)/shard_map/all_gather | solution.py:122
  143.1 2.4 %convolution_convert_fusion.1 = bf16[256,192]{0,1:T(8,128)(2,1)S(1)} fusion(bf16[256,3072]{1,0:T(8,128)(2,1)} %all-gather.2.cloned.1.call-done, bf16[3072,192]{0,1:T(8,128)(2,1)} %param.19), kind=kOutput, calls=%fused_computation.53 | convolution fusion | flops 302039040 | bytes 2850816 | tf_op jit(solution)/shard_map/dot_general | solution.py:121
  145.6 1.6 scatter_custom_fusion
  148.0 19.9 %all-to-all-start = ((bf16[128,2,192]{2,1,0:T(2,128)(2,1)}), bf16[128,2,192]{2,1,0:T(2,128)(2,1)S(1)}, u32[]{:S(2)}, u32[]{:S(2)}) async-start(bf16[128,2,192]{2,1,0:T(2,128)(2,1)} %all_to_all.14), calls=%async_computation | async-start | bytes 262144 | tf_op jit(solution)/shard_map/all_to_all | solution.py:129
  168.8 14.6 %all-to-all-done = bf16[128,2,192]{2,1,0:T(2,128)(2,1)S(1)} async-done(((bf16[128,2,192]{2,1,0:T(2,128)(2,1)}), bf16[128,2,192]{2,1,0:T(2,128)(2,1)S(1)}, u32[]{:S(2)}, u32[]{:S(2)}) %all-to-all-start) | async-done | bytes 98336 | tf_op jit(solution)/shard_map/all_to_all | solution.py:129
  (67 shorter events, 14.3 us)
Async XLA Ops:
  7.2 56.0 %copy-start = (bf16[768,1536]{1,0:T(8,128)(2,1)S(1)}, bf16[768,1536]{1,0:T(8,128)(2,1)}, u32[]{:S(2)}) copy-start(bf16[768,1536]{1,0:T(8,128)(2,1)} %param.15) | copy-start | bytes 7077892
  9.1 42.3 %all-to-all-start.1 = ((bf16[128,2,192]{2,1,0:T(2,128)(2,1)}), bf16[128,2,192]{2,1,0:T(2,128)(2,1)S(1)}, u32[]{:S(2)}, u32[]{:S(2)}) async-start(bf16[128,2,192]{2,1,0:T(2,128)(2,1)} %all_to_all.16), calls=%async_computation.1 | async-start | bytes 262144 | tf_op jit(solution)/shard_map/all_to_all | solution.py:130
  35.9 60.7 %reduce-scatter.2.cloned.1.call-start = ((), (), s32[]{:S(2)}) async-start(), calls=%async_computation.4 | async-start | bytes 1769472 | tf_op jit(solution)/shard_map/reduce_scatter | solution.py:132
  36.9 20.2 %collective-permute-start = (bf16[1,3,32,768]{3,2,1,0:T(8,128)(2,1)S(1)}, bf16[1,3,32,768]{3,2,1,0:T(8,128)(2,1)S(1)}, u32[]{:S(2)}, u32[]{:S(2)}) collective-permute-start(bf16[1,3,32,768]{3,2,1,0:T(8,128)(2,1)S(1)} %get-tuple-element.61), channel_id=1, source_target_pairs={{0,1},{1,2},{2,3},{3,4},{4,5},{5,6},{6,7},{8,9},{9,10},{10,11},{11... | collective-permute-start | bytes 442376 | tf_op jit(solution)/shard_map/ppermute | solution.py:17
  40.9 16.2 %collective-permute-start.1 = (bf16[1,3,32,768]{3,2,1,0:T(8,128)(2,1)S(1)}, bf16[1,3,32,768]{3,2,1,0:T(8,128)(2,1)S(1)}, u32[]{:S(2)}, u32[]{:S(2)}) collective-permute-start(bf16[1,3,32,768]{3,2,1,0:T(8,128)(2,1)S(1)} %get-tuple-element.62), channel_id=1, source_target_pairs={{1,0},{2,1},{3,2},{4,3},{5,4},{6,5},{7,6},{9,8},{10,9},{11,10},{12... | collective-permute-start | bytes 442376 | tf_op jit(solution)/shard_map/ppermute | solution.py:19
  45.5 10.3 %copy-start.6 = (s32[256,1]{0,1:T(1,128)}, s32[256,1]{0,1:T(1,128)S(1)}, u32[]{:S(2)}) copy-start(s32[256,1]{0,1:T(1,128)S(1)} %compare_select_fusion) | copy-start | bytes 3076
  52.6 4.5 %copy-start.1 = (bf16[1,4,32,768]{3,2,1,0:T(8,128)(2,1)S(1)}, bf16[1,4,32,768]{3,2,1,0:T(8,128)(2,1)}, u32[]{:S(2)}) copy-start(bf16[1,4,32,768]{3,2,1,0:T(8,128)(2,1)} %param.11) | copy-start | bytes 589828
  55.7 87.4 %all-gather.2.cloned.1.call-start = ((), (), s32[]{:S(2)}) async-start(), calls=%async_computation.3 | async-start | bytes 1769472 | tf_op jit(solution)/shard_map/all_gather | solution.py:122
  57.3 5.7 %copy-start.4 = (f32[768]{0:T(1024)S(1)}, f32[768]{0:T(1024)}, u32[]{:S(2)}) copy-start(f32[768]{0:T(1024)} %param.14) | copy-start | bytes 9220
  62.6 1.0 copy-start.11
  63.0 1.8 copy-start.10
  63.7 3.4 %copy-start.2 = (f32[128,1536]{1,0:T(8,128)}, f32[128,1536]{1,0:T(8,128)S(1)}, u32[]{:S(2)}) copy-start(f32[128,1536]{1,0:T(8,128)S(1)} %fusion.218) | copy-start | bytes 2359300
  67.0 33.7 %copy-start.3 = (f32[768]{0:T(1024)S(1)}, f32[768]{0:T(1024)}, u32[]{:S(2)}) copy-start(f32[768]{0:T(1024)} %param.18) | copy-start | bytes 9220
  67.0 0.7 copy-start.7
  97.9 12.3 %copy-start.5 = (f32[768]{0:T(1024)S(1)}, f32[768]{0:T(1024)}, u32[]{:S(2)}) copy-start(f32[768]{0:T(1024)} %param.14) | copy-start | bytes 9220
  114.5 53.4 %copy-start.8 = (f32[128]{0:T(128)S(1)}, f32[128]{0:T(128)}, u32[]{:S(2)}) copy-start(f32[128]{0:T(128)} %get-tuple-element.4) | copy-start | bytes 1540
  114.5 53.4 %copy-start.9 = (f32[128]{0:T(128)S(1)}, f32[128]{0:T(128)}, u32[]{:S(2)}) copy-start(f32[128]{0:T(128)} %get-tuple-element.5) | copy-start | bytes 1540
  148.0 35.4 %all-to-all-start = ((bf16[128,2,192]{2,1,0:T(2,128)(2,1)}), bf16[128,2,192]{2,1,0:T(2,128)(2,1)S(1)}, u32[]{:S(2)}, u32[]{:S(2)}) async-start(bf16[128,2,192]{2,1,0:T(2,128)(2,1)} %all_to_all.14), calls=%async_computation | async-start | bytes 262144 | tf_op jit(solution)/shard_map/all_to_all | solution.py:129
Sparse Core Ops, SparseCore 0:
  55.8 40.6 reduce-scatter.1
  108.3 34.7 all-gather.1
where the time goes:
time: 193 us; the launch traced here: 191 us
  waiting for transfers between devices  74.4 us (39%)
  starting transfers between devices  52.9 us (27%)
  local copies, waits for them, and re-layouts  24.3 us (13%)
  between operations  14.4 us (7%)
  other arithmetic  12.8 us (7%)
  matrix products  12.4 us (6%)
    reduce_scatter x1, waiting for transfers between devices, on_device(): lax.psum_scatter(lax.dot_general(grad_tokens, w_down, (((1,), (1,)), ((),...  28.8 us
    all_gather x1, waiting for transfers between devices, on_device(): lax.all_gather(patches, 'space', axis=0, tiled=True)  28.6 us
    all_to_all x1, starting transfers between devices, on_device(): lax.all_to_all(grad_packed[0], 'dp', split_axis=0, concat_axis=0, tiled=T...  26.8 us
    all_to_all x1, starting transfers between devices, on_device(): lax.all_to_all(send_buffer, 'dp', split_axis=0, concat_axis=0, tiled=True)  19.9 us
    all_to_all x1, waiting for transfers between devices, on_device(): lax.all_to_all(send_buffer, 'dp', split_axis=0, concat_axis=0, tiled=True)  14.6 us
    reduce_sum x1, other arithmetic, layer_norm(): center = values - jnp.mean(values, axis=-1, keepdims=True)  5.33 us
    slice x3, local copies, waits for them, and re-layouts, depthwise(): kernel[offset_y, offset_x]  4.69 us
    dot_general x1, matrix products, on_device(): lax.dot_general(grad_pre, w_expand, (((1,), (1,)), ((), ())), preferred_e...  4.32 us
  transfers between devices with their start and end apart: 6, of which 4 were waited for; matrix products, arithmetic and copies ran while one was open for 15% of the time, Pallas kernels for 0%

commit v1 on v0

v1 whole, which is shorter than its diff:
```python
import functools

import jax
import jax.numpy as jnp
from jax import lax
from jax.experimental import pallas as pl
from jax.experimental.pallas import tpu as pltpu
from jax.sharding import PartitionSpec as P

KS = 7
HALF = KS // 2
NY = 8
CORES = 2
CAP = 2
EPS = 1e-06
F32 = jnp.float32
BF16 = jnp.bfloat16
MESH = pl.DeviceIdType.MESH


def dot(a, b):
    return jnp.dot(a, b, preferred_element_type=F32)


def dot_nt(a, b):
    return lax.dot_general(a, b, (((1,), (1,)), ((), ())), preferred_element_type=F32)


def dot_tn(a, b):
    return lax.dot_general(a, b, (((0,), (0,)), ((), ())), preferred_element_type=F32)


def log2(n):
    return n.bit_length() - 1


def onehot(picked):
    return jnp.where(picked, 1.0, 0.0).astype(BF16)


def fields(index, *sizes):
    digits = []
    for size in reversed(sizes):
        digits.append(index & (size - 1))
        index = index >> log2(size)
    return digits[::-1]


def norm(v):
    center = v - jnp.mean(v, axis=-1, keepdims=True)
    inv = lax.rsqrt(jnp.mean(center * center, axis=-1, keepdims=True) + EPS)
    return center * inv, inv


def norm_back(grad, normed, inv, gain):
    h = grad * gain
    return inv * (
        h
        - jnp.mean(h, axis=-1, keepdims=True)
        - normed * jnp.mean(h * normed, axis=-1, keepdims=True)
    )


def kernel(
    dims,
    sec_h, dwk_h, bias_h, mixg_h, wexp_h, wred_h, scale_h, downg_h, wdt_h, owner_h, gpt_h,
    tok_o, grad_o,
    ext, dwk, bias, mixg, wexp, wred, scale, downg, wdt, owner, gpt,
    perm, pick, mid_f, mid_b, to_blocks, from_blocks,
    sgz, rgz, sgy, rgy, sty, rty, stz, rtz,
    mixed, normed1, inv1, firstn, firstp, resp, slope, hidden, gpre, proj, normed2, inv2,
    gathered, gtok, pair_s, pair_r, own_f, rs_s, rs_r, gsec, gscaled,
    load_sem, halo_ss, halo_rs, gz_ss, gz_rs, gy_ss, gy_rs, ty_ss, ty_rs, tz_ss, tz_rs,
    ag_ss, ag_rs, fw_ss, fw_rs, pair_ss, pair_rs, rs_ss, rs_rs,
):
    nz, nx, band, width, chans, hid, group, slots = dims
    n_space = nx * CORES
    rows = band * width
    tb = rows // 4
    zrows, yrows = NY * CAP, nz * CAP
    dp, sp = lax.axis_index("dp"), lax.axis_index("space")
    z, y = dp // NY, dp % NY
    x, core = sp // CORES, sp % CORES
    partner = x * CORES + (1 - core)

    def zdev(k):
        return ((z + k) % nz * NY + y, sp)

    def ydev(k):
        return (z * NY + (y + k) % NY, sp)

    def sdev(k):
        return (dp, (sp + k) % n_space)

    def xdev(k):
        return (dp, (x + k) % nx * CORES + core)

    pairs = [
        (sec_h, ext.at[HALF:HALF + band]), (gpt_h, gpt), (owner_h, owner), (dwk_h, dwk),
        (bias_h, bias), (mixg_h, mixg), (wexp_h, wexp), (wred_h, wred),
        (scale_h, scale), (downg_h, downg), (wdt_h, wdt),
    ]
    loads = [pltpu.make_async_copy(a, b, load_sem.at[i]) for i, (a, b) in enumerate(pairs)]
    for load in loads:
        load.start()

    barrier = pltpu.get_barrier_semaphore()

    def greet(count, device):
        @pl.loop(1, count)
        def _(k):
            pl.semaphore_signal(barrier, inc=1, device_id=device(k), device_id_type=MESH)

    greet(nz, zdev)
    greet(NY, ydev)
    greet(n_space, sdev)

    ii = lax.broadcasted_iota(jnp.int32, (slots, slots), 0)
    jj = lax.broadcasted_iota(jnp.int32, (slots, slots), 1)
    q_z, q_y, q_r = fields(ii, nz, NY, CAP)
    mid_f[...] = onehot(jj == q_y * yrows + q_z * CAP + q_r)
    p_y, p_z, p_r = fields(ii, NY, nz, CAP)
    mid_b[...] = onehot(jj == p_z * zrows + p_y * CAP + p_r)
    i2 = lax.broadcasted_iota(jnp.int32, (rows, rows), 0)
    j2 = lax.broadcasted_iota(jnp.int32, (rows, rows), 1)
    a, b, big_r, big_c = fields(i2, 2, 2, band // 2, width // 2)
    to_blocks[...] = onehot(j2 == (2 * big_r + a) * width + 2 * big_c + b)
    big_r, a, big_c, b = fields(i2, band // 2, 2, width // 2, 2)
    from_blocks[...] = onehot(j2 == ((a * 2 + b) * (band // 2) + big_r) * (width // 2) + big_c)

    loads[1].wait()
    sgz[...] = dot_nt(onehot(ii == jj), gpt[...]).astype(BF16)

    loads[2].wait()
    named = jnp.broadcast_to(owner[...].astype(F32), (slots, slots))
    named_col = jnp.sum(jnp.where(ii == jj, named, 0.0), axis=1, keepdims=True)
    rank = jnp.sum(
        jnp.where((named_col == named) & (ii < jj), 1.0, 0.0), axis=0, keepdims=True
    )
    o_z, o_y = fields(owner[...], nz, NY)
    pos = (o_y * yrows + o_z * CAP).astype(F32) + rank
    pos = jnp.broadcast_to(pos, (slots, slots))
    perm[...] = onehot(ii.astype(F32) == pos)
    u_core, u_x, u_i = fields(ii, CORES, nx, tb)
    pos_col = jnp.sum(
        jnp.where(jj == (u_x * CORES + u_core) * tb + u_i, pos, 0.0), axis=1, keepdims=True
    )
    pick[...] = onehot(jj.astype(F32) == pos_col)

    loads[0].wait()

    @pl.when(sp == 0)
    def _():
        ext[0:HALF] = jnp.zeros((HALF, width, chans), BF16)

    @pl.when(sp == n_space - 1)
    def _():
        ext[HALF + band:] = jnp.zeros((HALF, width, chans), BF16)

    pl.semaphore_wait(barrier, nz + NY + n_space - 3)

    def remote(src, dst, ss, rs, device):
        return pltpu.make_async_remote_copy(
            src_ref=src, dst_ref=dst, send_sem=ss, recv_sem=rs,
            device_id=device, device_id_type=MESH,
        )

    up = remote(
        ext.at[HALF:2 * HALF], ext.at[HALF + band:], halo_ss.at[0], halo_rs.at[0],
        (dp, jnp.maximum(sp - 1, 0)),
    )
    down = remote(
        ext.at[band:HALF + band], ext.at[0:HALF], halo_ss.at[1], halo_rs.at[1],
        (dp, jnp.minimum(sp + 1, n_space - 1)),
    )

    @pl.when(sp > 0)
    def _():
        up.start()

    @pl.when(sp < n_space - 1)
    def _():
        down.start()

    def block(k_index, size):
        return pl.ds(pl.multiple_of(k_index * size, size), size)

    def exchange(src, dst, ss, rs, count, me, size, device):
        def copy(k):
            return remote(
                src.at[block((me + k) % count, size)], dst.at[block(me, size)],
                ss.at[k], rs.at[k], device(k),
            )

        def begin():
            @pl.loop(1, count)
            def _(k):
                copy(k).start()

            dst[block(me, size)] = src[block(me, size)]

        def arrive():
            @pl.loop(1, count)
            def _(k):
                copy(k).wait_recv()

        def leave():
            @pl.loop(1, count)
            def _(k):
                copy(k).wait_send()

        return begin, arrive, leave

    gz = exchange(sgz, rgz, gz_ss, gz_rs, nz, z, zrows, zdev)
    gy = exchange(sgy, rgy, gy_ss, gy_rs, NY, y, yrows, ydev)
    ty = exchange(sty, rty, ty_ss, ty_rs, NY, y, yrows, ydev)
    tz = exchange(stz, rtz, tz_ss, tz_rs, nz, z, zrows, zdev)
    gz[0]()

    @pl.when(sp < n_space - 1)
    def _():
        up.wait_recv()

    @pl.when(sp > 0)
    def _():
        down.wait_recv()

    loads[3].wait()
    loads[4].wait()
    loads[5].wait()
    at = lax.broadcasted_iota(jnp.int32, (width, 128), 0)

    @pl.loop(0, chans // 128)
    def _(j):
        lanes = block(j, 128)

        @pl.loop(0, band)
        def _(r):
            acc = [None] * KS
            for dy in range(KS):
                line = ext[r + dy, :, lanes].astype(F32)
                for dx in range(KS):
                    term = line * dwk[dy, dx:dx + 1, lanes]
                    acc[dx] = term if dy == 0 else acc[dx] + term
            total = acc[HALF] + bias[:, lanes]
            for dx in range(KS):
                shift = dx - HALF
                if shift:
                    moved = pltpu.roll(acc[dx], -shift % width, 0)
                    inside = (at + shift >= 0) & (at + shift < width)
                    total = total + jnp.where(inside, moved, 0.0)
            mixed[block(r, width), lanes] = total

    @pl.loop(0, band)
    def _(r):
        at_rows = block(r, width)
        normed, inv = norm(mixed[at_rows, :])
        normed1[at_rows, :] = normed
        inv1[at_rows, :] = inv
        firstn[at_rows, :] = (normed * mixg[...]).astype(BF16)

    firstp[...] = dot(to_blocks[...], firstn[...]).astype(BF16)
    resp[...] = dot(to_blocks[...], ext[HALF:HALF + band].reshape(rows, chans))

    gz[1]()
    sgy[...] = dot(mid_b[...], rgz[...]).astype(BF16)
    gy[0]()

    loads[6].wait()

    @pl.loop(0, hid // 256)
    def _(j):
        cols = block(j, 256)
        pre = dot(firstp[...], wexp[:, cols])
        cumulative = 0.5 * (1.0 + lax.erf(pre * 0.7071067811865476))
        density = jnp.exp(-0.5 * pre * pre) * 0.3989422804014327
        hidden[:, cols] = (pre * cumulative).astype(BF16)
        slope[:, cols] = cumulative + pre * density

    loads[7].wait()

    @pl.loop(0, chans // 256)
    def _(j):
        cols = block(j, 256)
        proj[:, cols] = dot(hidden[...], wred[:, cols])

    loads[8].wait()
    loads[9].wait()
    for q in range(4):
        at_rows = slice(q * tb, (q + 1) * tb)
        normed, inv = norm(resp[at_rows, :] + scale[...] * proj[at_rows, :])
        normed2[at_rows, :] = normed
        inv2[at_rows, :] = inv
        gathered[block(sp, tb), q * chans:(q + 1) * chans] = (normed * downg[...]).astype(BF16)

    def ag(k):
        own = gathered.at[block(sp, tb)]
        return remote(own, own, ag_ss.at[k], ag_rs.at[k], xdev(k))

    def forward(k):
        held = gathered.at[block((x + nx - k) % nx * CORES + core, tb)]
        return remote(held, held, fw_ss.at[k], fw_rs.at[k], (dp, partner))

    for k in range(1, nx):
        ag(k).start()
    forward(0).start()

    gy[1]()
    gtok[...] = dot(pick[...], rgy[...]).astype(BF16)
    loads[10].wait()
    half = nx * tb

    @pl.loop(0, 4 * chans // 512)
    def _(j):
        cols = block(j, 512)
        pair_s[:, cols] = dot(gtok[block(1 - core, half), :], wdt[:, cols]).astype(BF16)

    pair = remote(pair_s, pair_r, pair_ss, pair_rs, (dp, partner))
    pair.start()

    @pl.loop(0, 4 * chans // 512)
    def _(j):
        cols = block(j, 512)
        own_f[:, cols] = dot(gtok[block(core, half), :], wdt[:, cols])

    for k in range(1, nx):
        ag(k).wait_recv()
        forward(k).start()
    pair.wait_recv()

    def scatter(k):
        return remote(
            rs_s.at[block(k, tb)], rs_r.at[block(k, tb)], rs_ss.at[k], rs_rs.at[k], xdev(k)
        )

    for k in range(1, nx):
        there = block((x + k) % nx, tb)
        rs_s[k * tb:(k + 1) * tb, :] = (own_f[there, :] + pair_r[there, :].astype(F32)).astype(BF16)
        scatter(k).start()

    for k in range(nx):
        forward(k).wait_recv()
    tokens = dot_nt(gathered[:, 0:chans], wdt[:, 0:chans])
    for q in range(1, 4):
        cols = slice(q * chans, (q + 1) * chans)
        tokens = tokens + dot_nt(gathered[:, cols], wdt[:, cols])
    sty[...] = dot(perm[...], tokens.astype(BF16)).astype(BF16)
    ty[0]()

    for k in range(1, nx):
        scatter(k).wait_recv()
    here = block(x, tb)
    for q in range(4):
        cols = slice(q * chans, (q + 1) * chans)
        at_rows = slice(q * tb, (q + 1) * tb)
        grad = own_f[here, cols] + pair_r[here, cols].astype(F32)
        for k in range(1, nx):
            grad = grad + rs_r[k * tb:(k + 1) * tb, cols].astype(F32)
        grad = norm_back(grad, normed2[at_rows, :], inv2[at_rows, :], downg[...])
        gscaled[at_rows, :] = (grad * scale[...]).astype(BF16)

    ty[1]()
    stz[...] = dot(mid_f[...], rty[...]).astype(BF16)
    tz[0]()

    @pl.loop(0, hid // 256)
    def _(j):
        cols = block(j, 256)
        grad = dot_nt(gscaled[...], wred[cols, :]) * slope[:, cols]
        gpre[:, cols] = dot(from_blocks[...], grad.astype(BF16)).astype(BF16)

    @pl.loop(0, chans // 256)
    def _(j):
        cols = block(j, 256)
        gsec[:, cols] = dot_nt(gpre[...], wexp[cols, :])

    @pl.loop(0, band)
    def _(r):
        at_rows = block(r, width)
        grad = norm_back(gsec[at_rows, :], normed1[at_rows, :], inv1[at_rows, :], mixg[...])
        grad_o[at_rows, :] = grad.astype(BF16)

    tz[1]()
    tok_o[...] = dot_tn(rtz[...], onehot(ii == jj)).astype(BF16)

    @pl.when(sp > 0)
    def _():
        up.wait_send()

    @pl.when(sp < n_space - 1)
    def _():
        down.wait_send()

    for k in range(1, nx):
        ag(k).wait_send()
        scatter(k).wait_send()
    for k in range(nx):
        forward(k).wait_send()
    pair.wait_send()
    for phase in (gz, gy, ty, tz):
        phase[2]()


def on_device(
    section_three, dw_kernel, dw_bias, mix_gain, w_expand, w_reduce, layer_scale, down_gain,
    w_down, owner_table, grad_packed,
):
    _, band, width, chans = section_three.shape
    hid = w_expand.shape[1]
    group = w_down.shape[1]
    slots = grad_packed.shape[1]
    n_dp, n_space = lax.axis_size("dp"), lax.axis_size("space")
    nz, nx = n_dp // NY, n_space // CORES
    rows = band * width
    tb = rows // 4
    dims = (nz, nx, band, width, chans, hid, group, slots)
    vmem = pltpu.VMEM
    dma = pltpu.SemaphoreType.DMA
    scratch = [
        vmem((band + 2 * HALF, width, chans), BF16),
        vmem((KS, KS, chans), F32), vmem((1, chans), F32), vmem((1, chans), F32),
        vmem((chans, hid), BF16), vmem((hid, chans), BF16), vmem((1, chans), F32),
        vmem((1, chans), F32), vmem((group, 4 * chans), BF16), vmem((1, slots), jnp.int32),
        vmem((group, slots), BF16),
        *[vmem((slots, slots), BF16)] * 4, *[vmem((rows, rows), BF16)] * 2,
        *[vmem((slots, group), BF16)] * 8,
        vmem((rows, chans), F32), vmem((rows, chans), F32), vmem((rows, 1), F32),
        vmem((rows, chans), BF16), vmem((rows, chans), BF16), vmem((rows, chans), F32),
        vmem((rows, hid), F32), vmem((rows, hid), BF16), vmem((rows, hid), BF16),
        vmem((rows, chans), F32), vmem((rows, chans), F32), vmem((rows, 1), F32),
        vmem((n_space * tb, 4 * chans), BF16), vmem((slots, group), BF16),
        vmem((nx * tb, 4 * chans), BF16), vmem((nx * tb, 4 * chans), BF16),
        vmem((nx * tb, 4 * chans), F32),
        vmem((nx * tb, 4 * chans), BF16), vmem((nx * tb, 4 * chans), BF16),
        vmem((rows, chans), F32), vmem((rows, chans), BF16),
        dma((11,)), dma((2,)), dma((2,)),
        dma((nz,)), dma((nz,)), dma((NY,)), dma((NY,)),
        dma((NY,)), dma((NY,)), dma((nz,)), dma((nz,)),
        dma((nx,)), dma((nx,)), dma((nx,)), dma((nx,)), dma, dma, dma((nx,)), dma((nx,)),
    ]
    anywhere = pl.BlockSpec(memory_space=pl.ANY)
    inside = pl.BlockSpec(memory_space=pltpu.VMEM)
    macs = rows * chans * hid * 4 + 2 * slots * group * 4 * chans
    tok, grad = pl.pallas_call(
        functools.partial(kernel, dims),
        out_shape=(
            jax.ShapeDtypeStruct((group, slots), BF16),
            jax.ShapeDtypeStruct((rows, chans), BF16),
        ),
        in_specs=[anywhere] * 11,
        out_specs=(inside, inside),
        scratch_shapes=scratch,
        compiler_params=pltpu.CompilerParams(
            collective_id=0, has_side_effects=True, vmem_limit_bytes=56 * 2**20
        ),
        cost_estimate=pl.CostEstimate(
            flops=2 * macs, bytes_accessed=8 * 2**20, transcendentals=2 * rows * hid
        ),
    )(
        section_three[0], dw_kernel, dw_bias[None], mix_gain[None], w_expand, w_reduce,
        layer_scale[None], down_gain[None], w_down.T, owner_table[:, :, 0], grad_packed[0].T,
    )
    return tok.T[None], grad.reshape(1, band, width, chans)


def solution(mesh):
    in_specs = (
        P("dp", "space", None, None), P(), P(), P(), P(), P(), P(), P(), P(None, "space"),
        P("dp", None, None), P("dp", None, "space"),
    )
    out_specs = (P("dp", None, "space"), P("dp", "space", None, None))
    return jax.shard_map(
        on_device, mesh=mesh, in_specs=in_specs, out_specs=out_specs, check_vma=False
    )
```

time: 193 us -> 77.9 us (0.40)
  waiting for transfers between devices: 74.4 us -> 0 us
  Pallas kernels: 0 us -> 68.7 us
  starting transfers between devices: 52.9 us -> 0 us
  local copies, waits for them, and re-layouts: 24.3 us -> 8.24 us
  between operations: 14.4 us -> 0.64 us
  other arithmetic: 12.8 us -> 0 us
  matrix products: 12.4 us -> 0 us
    pallas_call x0 -> x1, Pallas kernels: none -> 68.7 us  [on_device(): pl.pallas_call(functools.partial(kernel, dims), out_shape=(jax.ShapeDtype...]
    all_to_all x2 -> x0, starting transfers between devices: 46.7 us -> none  [the longest x1 26.8 us: on_device(): lax.all_to_all(grad_packed[0], 'dp', split_axis=0, concat_axis=0, tiled=T...]
    reduce_scatter x1 -> x0, waiting for transfers between devices: 28.8 us -> none  [on_device(): lax.psum_scatter(lax.dot_general(grad_tokens, w_down, (((1,), (1,)), ((),...]
    all_gather x1 -> x0, waiting for transfers between devices: 28.6 us -> none  [on_device(): lax.all_gather(patches, 'space', axis=0, tiled=True)]
    all_to_all x2 -> x0, waiting for transfers between devices: 17 us -> none  [the longest x1 14.6 us: on_device(): lax.all_to_all(send_buffer, 'dp', split_axis=0, concat_axis=0, tiled=True)]
    dot_general x5 -> x0, matrix products: 12.4 us -> none  [the longest x1 4.32 us: on_device(): lax.dot_general(grad_pre, w_expand, (((1,), (1,)), ((), ())), preferred_e...]
    reduce_sum x6 -> x0, other arithmetic: 9.09 us -> none  [the longest x1 5.33 us: layer_norm(): center = values - jnp.mean(values, axis=-1, keepdims=True)]
    ppermute x2 -> x0, starting transfers between devices: 5.88 us -> none  [the longest x1 3.96 us: padded_2(): lax.ppermute(tail, axis, [(i, (i + 1) % count) for i in range(ends)])]
  transfers between devices with their start and end apart: 6 -> 0, of which waited for: 4 -> 0; matrix products, arithmetic and copies ran while one was open for 15% -> 0% of each run, Pallas kernels for 0% -> 0%
where the time goes in v1:
time: 77.9 us; the launch traced here: 77.6 us
  Pallas kernels  68.7 us (88%)
  local copies, waits for them, and re-layouts  8.24 us (11%)
    pallas_call x1, Pallas kernels, on_device(): pl.pallas_call(functools.partial(kernel, dims), out_shape=(jax.ShapeDtype...  68.7 us
    unnamed x2, local copies, waits for them, and re-layouts  3.16 us

profile of v1, /device:TPU:1, one launch (start us, length us, event | category | flops | bytes accessed | tf_op | source)
XLA Modules:
  0.0 77.6 jit_solution(8938140750930000592)
XLA Ops:
  0.6 1.3 %broadcast_in_dim.15.bias_h = f32[1,768]{1,0:T(1,128)} reshape(f32[768]{0:T(1024)} %param.13) | data formatting | bytes 6144 | tf_op jit(solution)/shard_map/broadcast_in_dim | solution.py:460
  1.9 1.3 %broadcast_in_dim.16.mixg_h = f32[1,768]{1,0:T(1,128)} reshape(f32[768]{0:T(1024)} %param.14) | data formatting | bytes 6144 | tf_op jit(solution)/shard_map/broadcast_in_dim | solution.py:460
  3.2 1.3 %broadcast_in_dim.17.scale_h = f32[1,768]{1,0:T(1,128)} reshape(f32[768]{0:T(1024)} %param.17) | data formatting | bytes 6144 | tf_op jit(solution)/shard_map/broadcast_in_dim | solution.py:461
  4.4 1.3 %broadcast_in_dim.18.downg_h = f32[1,768]{1,0:T(1,128)} reshape(f32[768]{0:T(1024)} %param.18) | data formatting | bytes 6144 | tf_op jit(solution)/shard_map/broadcast_in_dim | solution.py:461
  5.7 68.7 %shard_map.122 = (bf16[192,256]{1,0:T(8,128)(2,1)}, bf16[128,768]{1,0:T(8,128)(2,1)}) custom-call(bf16[4,32,768]{2,1,0:T(8,128)(2,1)} %bitcast.13, f32[7,7,768]{2,1,0:T(8,128)} %dwk_h.1, f32[1,768]{1,0:T(1,128)} %broadcast_in_dim.15.bias_h, f32[1,768]{1,0:T(1,128)} %broadcast_in_dim.16.mixg_h, bf16[768,1536]{1,0:T(8,128)(2,1)} %wexp_h.1, ...), custom_call_target="tpu_custom_call" | custom-call | flops 1811939328 | bytes 8388608 | tf_op jit(solution)/shard_map/pallas_call | solution.py:444
  74.4 1.5 %copy.15 = bf16[1,256,192]{1,2,0:T(8,128)(2,1)} copy(bf16[1,256,192]{1,2,0:T(8,128)(2,1)} %bitcast.11) | data formatting | bytes 196608
  76.0 1.6 %copy.16 = bf16[1,4,32,768]{3,2,1,0:T(8,128)(2,1)} copy(bf16[1,4,32,768]{3,2,1,0:T(8,128)(2,1)} %bitcast.10) | data formatting | bytes 393216

commit v2 on v1

v2 whole, which is shorter than its diff:
```python
import functools

import jax
import jax.numpy as jnp
from jax import lax
from jax.experimental import pallas as pl
from jax.experimental.pallas import tpu as pltpu
from jax.sharding import PartitionSpec as P

KS = 7
HALF = KS // 2
NY = 8
CORES = 2
CAP = 2
EPS = 1e-06
F32 = jnp.float32
BF16 = jnp.bfloat16
MESH = pl.DeviceIdType.MESH


def dot(a, b):
    return jnp.dot(a, b, preferred_element_type=F32)


def dot_nt(a, b):
    return lax.dot_general(a, b, (((1,), (1,)), ((), ())), preferred_element_type=F32)


def dot_tn(a, b):
    return lax.dot_general(a, b, (((0,), (0,)), ((), ())), preferred_element_type=F32)


def log2(n):
    return n.bit_length() - 1


def onehot(picked):
    return jnp.where(picked, 1.0, 0.0).astype(BF16)


def fields(index, *sizes):
    digits = []
    for size in reversed(sizes):
        digits.append(index & (size - 1))
        index = index >> log2(size)
    return digits[::-1]


def norm(v):
    center = v - jnp.mean(v, axis=-1, keepdims=True)
    inv = lax.rsqrt(jnp.mean(center * center, axis=-1, keepdims=True) + EPS)
    return center * inv, inv


def norm_back(grad, normed, inv, gain):
    h = grad * gain
    return inv * (
        h
        - jnp.mean(h, axis=-1, keepdims=True)
        - normed * jnp.mean(h * normed, axis=-1, keepdims=True)
    )


def kernel(
    dims,
    sec_h, dwk_h, bias_h, mixg_h, wexp_h, wred_h, scale_h, downg_h, wdt_h, owner_h, gpt_h,
    tok_o, grad_o,
    ext, dwk, bias, mixg, wexp, wred, scale, downg, wdt, owner, gpt,
    perm, pick, mid_b,
    sgz, rgz, sgy, rgy, st, rt,
    mixed, normed1, inv1, first, slope, hidden, gpre, proj, normed2, inv2, second,
    gathered, gtok, pair_s, pair_r, own_f, rs_s, rs_r, gfirst, gscaled,
    load_sem, halo_ss, halo_rs, gz_ss, gz_rs, gy_ss, gy_rs, t_ss, t_rs,
    ag_ss, ag_rs, fw_ss, fw_rs, pair_ss, pair_rs, rs_ss, rs_rs,
):
    nz, nx, band, width, chans, hid, group, slots = dims
    n_space = nx * CORES
    rows = band * width
    tb = rows // 4
    zrows, yrows = NY * CAP, nz * CAP
    dp, sp = lax.axis_index("dp"), lax.axis_index("space")
    z, y = dp // NY, dp % NY
    x, core = sp // CORES, sp % CORES
    partner = x * CORES + (1 - core)

    def zdev(k):
        return ((z + k) % nz * NY + y, sp)

    def ydev(k):
        return (z * NY + (y + k) % NY, sp)

    def sdev(k):
        return (dp, (sp + k) % n_space)

    def xdev(k):
        return (dp, (x + k) % nx * CORES + core)

    barrier = pltpu.get_barrier_semaphore()

    def greet(count, device):
        @pl.loop(1, count)
        def _(k):
            pl.semaphore_signal(barrier, inc=1, device_id=device(k), device_id_type=MESH)

    greet(n_space, sdev)
    greet(nz, zdev)
    greet(NY, ydev)

    pairs = [
        (sec_h, ext.at[HALF:HALF + band]), (gpt_h, gpt), (owner_h, owner), (dwk_h, dwk),
        (bias_h, bias.at[0]), (mixg_h, mixg.at[0]), (wexp_h, wexp), (wred_h, wred),
        (scale_h, scale.at[0]), (downg_h, downg.at[0]), (wdt_h, wdt),
    ]
    loads = [pltpu.make_async_copy(a, b, load_sem.at[i]) for i, (a, b) in enumerate(pairs)]
    for load in loads:
        load.start()

    ii = lax.broadcasted_iota(jnp.int32, (slots, slots), 0)
    jj = lax.broadcasted_iota(jnp.int32, (slots, slots), 1)
    p_y, p_z, p_r = fields(ii, NY, nz, CAP)
    mid_b[...] = onehot(jj == p_z * zrows + p_y * CAP + p_r)
    loads[1].wait()
    sgz[...] = dot_nt(onehot(ii == jj), gpt[...]).astype(BF16)

    loads[2].wait()
    named = jnp.broadcast_to(owner[...].astype(F32), (slots, slots))
    named_col = jnp.sum(jnp.where(ii == jj, named, 0.0), axis=1, keepdims=True)
    rank = jnp.sum(
        jnp.where((named_col == named) & (ii < jj), 1.0, 0.0), axis=0, keepdims=True
    )
    slot = jnp.broadcast_to((owner[...] * CAP).astype(F32) + rank, (slots, slots))
    perm[...] = onehot(ii.astype(F32) == slot)
    o_z, o_y = fields(owner[...], nz, NY)
    pos = (o_y * yrows + o_z * CAP).astype(F32) + rank
    pos = jnp.broadcast_to(pos, (slots, slots))
    u_core, u_x, u_i = fields(ii, CORES, nx, tb)
    pos_col = jnp.sum(
        jnp.where(jj == (u_x * CORES + u_core) * tb + u_i, pos, 0.0), axis=1, keepdims=True
    )
    pick[...] = onehot(jj.astype(F32) == pos_col)

    loads[0].wait()

    @pl.when(sp == 0)
    def _():
        ext[0:HALF] = jnp.zeros((HALF, width, chans), BF16)

    @pl.when(sp == n_space - 1)
    def _():
        ext[HALF + band:] = jnp.zeros((HALF, width, chans), BF16)

    pl.semaphore_wait(barrier, nz + NY + n_space - 3)

    def remote(src, dst, ss, rs, device):
        return pltpu.make_async_remote_copy(
            src_ref=src, dst_ref=dst, send_sem=ss, recv_sem=rs,
            device_id=device, device_id_type=MESH,
        )

    up = remote(
        ext.at[HALF:2 * HALF], ext.at[HALF + band:], halo_ss.at[0], halo_rs.at[0],
        (dp, jnp.maximum(sp - 1, 0)),
    )
    down = remote(
        ext.at[band:HALF + band], ext.at[0:HALF], halo_ss.at[1], halo_rs.at[1],
        (dp, jnp.minimum(sp + 1, n_space - 1)),
    )

    @pl.when(sp > 0)
    def _():
        up.start()

    @pl.when(sp < n_space - 1)
    def _():
        down.start()

    def block(k_index, size):
        return pl.ds(pl.multiple_of(k_index * size, size), size)

    def exchange(src, dst, ss, rs, count, me, size, device):
        def copy(k):
            return remote(
                src.at[block((me + k) % count, size)], dst.at[block(me, size)],
                ss.at[k], rs.at[k], device(k),
            )

        def begin():
            @pl.loop(1, count)
            def _(k):
                copy(k).start()

            dst[block(me, size)] = src[block(me, size)]

        def arrive():
            @pl.loop(1, count)
            def _(k):
                copy(k).wait_recv()

        def leave():
            @pl.loop(1, count)
            def _(k):
                copy(k).wait_send()

        return begin, arrive, leave

    gz = exchange(sgz, rgz, gz_ss, gz_rs, nz, z, zrows, zdev)
    gy = exchange(sgy, rgy, gy_ss, gy_rs, NY, y, yrows, ydev)
    gz[0]()

    for i in (3, 4, 5):
        loads[i].wait()
    at = lax.broadcasted_iota(jnp.int32, (width, 128), 0)

    def convolve(r, lanes, count, source):
        acc = [None] * KS
        for i in range(count):
            e = source(r, i)
            line = ext[e, :, lanes].astype(F32)
            taps = dwk[e - r, :, lanes]
            for dx in range(KS):
                term = line * taps[dx:dx + 1]
                acc[dx] = term if i == 0 else acc[dx] + term
        total = acc[HALF]
        for dx in range(KS):
            shift = dx - HALF
            if shift:
                moved = pltpu.roll(acc[dx], -shift % width, 0)
                inside = (at + shift >= 0) & (at + shift < width)
                total = total + jnp.where(inside, moved, 0.0)
        return total

    @pl.loop(0, chans // 128)
    def _(j):
        lanes = block(j, 128)

        @pl.loop(0, band)
        def _(r):
            own = convolve(r, lanes, band, lambda r, i: HALF + i)
            mixed[block(r, width), lanes] = own + bias[:, lanes]

    @pl.when(sp < n_space - 1)
    def _():
        up.wait_recv()

    @pl.when(sp > 0)
    def _():
        down.wait_recv()

    @pl.loop(0, chans // 128)
    def _(j):
        lanes = block(j, 128)

        @pl.loop(0, band)
        def _(r):
            at_rows = block(r, width)
            mixed[at_rows, lanes] += convolve(
                r, lanes, HALF, lambda r, i: r + i + band * ((r + i) // HALF)
            )

    @pl.loop(0, band)
    def _(r):
        at_rows = block(r, width)
        normed, inv = norm(mixed[at_rows, :])
        normed1[at_rows, :] = normed
        inv1[at_rows, :] = inv
        first[at_rows, :] = (normed * mixg[...]).astype(BF16)

    loads[6].wait()

    @pl.loop(0, hid // 256)
    def _(j):
        cols = block(j, 256)
        pre = dot(first[...], wexp[:, cols])
        cumulative = 0.5 * (1.0 + lax.erf(pre * 0.7071067811865476))
        density = jnp.exp(-0.5 * pre * pre) * 0.3989422804014327
        hidden[:, cols] = (pre * cumulative).astype(BF16)
        slope[:, cols] = cumulative + pre * density

    loads[7].wait()

    @pl.loop(0, chans // 256)
    def _(j):
        cols = block(j, 256)
        proj[:, cols] = dot(hidden[...], wred[:, cols])

    loads[8].wait()
    loads[9].wait()

    @pl.loop(0, band)
    def _(r):
        at_rows = block(r, width)
        residual = ext[HALF + r].astype(F32)
        normed, inv = norm(residual + scale[...] * proj[at_rows, :])
        inv2[at_rows, :] = jnp.broadcast_to(inv, (width, 128))
        for c in range(chans // 128):
            lanes = slice(c * 128, (c + 1) * 128)
            normed2[c, at_rows, :] = normed[:, lanes]
            second[c, at_rows, :] = normed[:, lanes] * downg[:, lanes]

    def spots(a, b, big_r):
        return pl.ds((2 * big_r + a) * width + b, width // 2, stride=2)

    for a in range(2):
        for b in range(2):
            for c in range(chans // 128):
                lanes = slice((2 * a + b) * chans + c * 128, (2 * a + b) * chans + (c + 1) * 128)
                lines = [second[c, spots(a, b, big_r), :] for big_r in range(band // 2)]
                gathered[block(sp, tb), lanes] = jnp.concatenate(lines, axis=0).astype(BF16)

    right, left, over = (x + 1) % nx, (x + nx - 1) % nx, (x + 2) % nx

    def held(chip, h):
        return gathered.at[pl.ds(pl.multiple_of((chip * CORES + core) * tb + h * (tb // 2), tb // 2), tb // 2)]

    def ag(i, chip, h, target):
        return remote(
            held(chip, h), held(chip, h), ag_ss.at[i], ag_rs.at[i], (dp, target * CORES + core)
        )

    def fw(i, chip, h):
        return remote(held(chip, h), held(chip, h), fw_ss.at[i], fw_rs.at[i], (dp, partner))

    sends = [
        ag(0, x, 0, right), ag(1, x, 1, left), ag(2, x, 1, right), ag(3, x, 0, left),
        ag(4, left, 0, right), ag(5, right, 1, left),
    ]
    passed = [
        fw(0, left, 0), fw(1, right, 1), fw(2, left, 1), fw(3, right, 0),
        fw(4, over, 0), fw(5, over, 1), fw(6, x, 0), fw(7, x, 1),
    ]
    for i in range(4):
        sends[i].start()
    passed[6].start()
    passed[7].start()

    gz[1]()
    sgy[...] = dot(mid_b[...], rgz[...]).astype(BF16)
    gy[0]()

    for i in range(4):
        sends[i].wait_recv()
        if i < 2:
            sends[4 + i].start()
        passed[i].start()

    gy[1]()
    gtok[...] = dot(pick[...], rgy[...]).astype(BF16)
    loads[10].wait()
    half = nx * tb
    parts = [slice(q * chans, (q + 1) * chans) for q in range(4)]

    def pair(q):
        return remote(pair_s.at[q], pair_r.at[q], pair_ss.at[q], pair_rs.at[q], (dp, partner))

    def scatter(q, k):
        to = pl.ds(k * tb, tb)
        return remote(
            rs_s.at[q, to], rs_r.at[q, to], rs_ss.at[q, k], rs_rs.at[q, k], xdev(k)
        )

    for q in range(4):
        pair_s[q] = dot(gtok[block(1 - core, half), :], wdt[:, parts[q]]).astype(BF16)
        pair(q).start()

    for i in range(4, 6):
        sends[i].wait_recv()
        passed[i].start()

    for q in range(4):
        own_f[q] = dot(gtok[block(core, half), :], wdt[:, parts[q]])
        pair(q).wait_recv()
        for k in (2, 1, 3):
            there = block((x + k) % nx, tb)
            rs_s[q, k * tb:(k + 1) * tb, :] = (
                own_f[q, there, :] + pair_r[q, there, :].astype(F32)
            ).astype(BF16)
            scatter(q, k).start()

    for copy in passed:
        copy.wait_recv()
    tokens = dot_nt(gathered[:, 0:chans], wdt[:, 0:chans])
    for q in range(1, 4):
        cols = slice(q * chans, (q + 1) * chans)
        tokens = tokens + dot_nt(gathered[:, cols], wdt[:, cols])
    st[...] = dot(perm[...], tokens.astype(BF16)).astype(BF16).reshape(slots // CAP, CAP, group)

    def token(far_y, far_z):
        def away(far, count):
            return (count // 2 + (1 - 2 * (far % 2)) * ((far + 1) // 2) + count) % count

        o = (z + away(far_z, nz)) % nz * NY + (y + away(far_y, NY)) % NY
        remote(st.at[o], rt.at[dp], t_ss, t_rs, (o, sp)).start()

    @pl.loop(0, NY - 1)
    def _(far_y):
        @pl.loop(0, nz, unroll=nz)
        def _(far_z):
            token(far_y, far_z)

    @pl.loop(0, nz - 1, unroll=nz - 1)
    def _(far_z):
        token(NY - 1, far_z)

    rt[dp] = st[dp]

    here = block(x, tb)
    gain = downg[...]
    for a in range(2):
        for b in range(2):
            q = 2 * a + b
            grad = own_f[q, here, :] + pair_r[q, here, :].astype(F32)
            for k in (1, 3, 2):
                scatter(q, k).wait_recv()
                grad = grad + rs_r[q, k * tb:(k + 1) * tb, :].astype(F32)
            normed = jnp.concatenate([
                jnp.concatenate(
                    [normed2[c, spots(a, b, big_r), :] for c in range(chans // 128)], axis=1
                ) for big_r in range(band // 2)
            ], axis=0)
            inv = jnp.concatenate(
                [inv2[spots(a, b, big_r), :] for big_r in range(band // 2)], axis=0
            )
            grad = norm_back(grad, normed, inv[:, 0:1], gain) * scale[...]
            for big_r in range(band // 2):
                for c in range(chans // 128):
                    second[c, spots(a, b, big_r), :] = grad[
                        big_r * (width // 2):(big_r + 1) * (width // 2), c * 128:(c + 1) * 128
                    ]
    for c in range(chans // 128):
        gscaled[:, c * 128:(c + 1) * 128] = second[c].astype(BF16)

    @pl.loop(0, hid // 256)
    def _(j):
        cols = block(j, 256)
        gpre[:, cols] = (dot_nt(gscaled[...], wred[cols, :]) * slope[:, cols]).astype(BF16)

    @pl.loop(0, chans // 256)
    def _(j):
        cols = block(j, 256)
        gfirst[:, cols] = dot_nt(gpre[...], wexp[cols, :])

    @pl.loop(0, band)
    def _(r):
        at_rows = block(r, width)
        grad = norm_back(gfirst[at_rows, :], normed1[at_rows, :], inv1[at_rows, :], mixg[...])
        grad_o[at_rows, :] = grad.astype(BF16)

    every = slots // CAP - 1
    came = remote(st.at[0:every], rt.at[0:every], t_ss, t_rs, (dp, partner))
    came.wait_recv()
    tok_o[...] = dot_tn(rt[...].reshape(slots, group), onehot(ii == jj)).astype(BF16)

    @pl.when(sp > 0)
    def _():
        up.wait_send()

    @pl.when(sp < n_space - 1)
    def _():
        down.wait_send()

    for q in range(4):
        pair(q).wait_send()
        for k in range(1, nx):
            scatter(q, k).wait_send()
    for copy in (*sends, *passed):
        copy.wait_send()
    came.wait_send()
    for phase in (gz, gy):
        phase[2]()


def on_device(
    section_three, dw_kernel, dw_bias, mix_gain, w_expand, w_reduce, layer_scale, down_gain,
    w_down, owner_table, grad_packed,
):
    _, band, width, chans = section_three.shape
    hid = w_expand.shape[1]
    group = w_down.shape[1]
    slots = grad_packed.shape[1]
    n_dp, n_space = lax.axis_size("dp"), lax.axis_size("space")
    nz, nx = n_dp // NY, n_space // CORES
    rows = band * width
    tb = rows // 4
    dims = (nz, nx, band, width, chans, hid, group, slots)
    vmem = pltpu.VMEM
    dma = pltpu.SemaphoreType.DMA
    scratch = [
        vmem((band + 2 * HALF, width, chans), BF16),
        vmem((KS, KS, chans), F32), vmem((1, chans), F32), vmem((1, chans), F32),
        vmem((chans, hid), BF16), vmem((hid, chans), BF16), vmem((1, chans), F32),
        vmem((1, chans), F32), vmem((group, 4 * chans), BF16), vmem((1, slots), jnp.int32),
        vmem((group, slots), BF16),
        *[vmem((slots, slots), BF16)] * 3,
        *[vmem((slots, group), BF16)] * 4, *[vmem((slots // CAP, CAP, group), BF16)] * 2,
        vmem((rows, chans), F32), vmem((rows, chans), F32), vmem((rows, 1), F32),
        vmem((rows, chans), BF16), vmem((rows, hid), F32), vmem((rows, hid), BF16),
        vmem((rows, hid), BF16), vmem((rows, chans), F32),
        vmem((chans // 128, rows, 128), F32), vmem((rows, 128), F32),
        vmem((chans // 128, rows, 128), F32),
        vmem((n_space * tb, 4 * chans), BF16), vmem((slots, group), BF16),
        vmem((4, nx * tb, chans), BF16), vmem((4, nx * tb, chans), BF16),
        vmem((4, nx * tb, chans), F32),
        vmem((4, nx * tb, chans), BF16), vmem((4, nx * tb, chans), BF16),
        vmem((rows, chans), F32), vmem((rows, chans), BF16),
        dma((11,)), dma((2,)), dma((2,)),
        dma((nz,)), dma((nz,)), dma((NY,)), dma((NY,)),
        dma, dma, dma((6,)), dma((6,)), dma((8,)), dma((8,)), dma((4,)), dma((4,)),
        dma((4, nx)), dma((4, nx)),
    ]
    anywhere = pl.BlockSpec(memory_space=pl.ANY)
    inside = pl.BlockSpec(memory_space=pltpu.VMEM)
    macs = rows * chans * hid * 4 + 2 * slots * group * 4 * chans
    tok, grad = pl.pallas_call(
        functools.partial(kernel, dims),
        out_shape=(vmem((group, slots), BF16), vmem((rows, chans), BF16)),
        in_specs=[anywhere] * 11,
        out_specs=(inside, inside),
        scratch_shapes=scratch,
        compiler_params=pltpu.CompilerParams(
            collective_id=0, has_side_effects=True, vmem_limit_bytes=56 * 2**20
        ),
        cost_estimate=pl.CostEstimate(
            flops=2 * macs, bytes_accessed=8 * 2**20, transcendentals=2 * rows * hid
        ),
    )(
        section_three[0], dw_kernel, dw_bias, mix_gain, w_expand, w_reduce,
        layer_scale, down_gain, w_down.T, owner_table[:, :, 0], grad_packed[0].T,
    )
    return tok.T[None], grad.reshape(1, band, width, chans)


def solution(mesh):
    in_specs = (
        P("dp", "space", None, None), P(), P(), P(), P(), P(), P(), P(), P(None, "space"),
        P("dp", None, None), P("dp", None, "space"),
    )
    out_specs = (P("dp", None, "space"), P("dp", "space", None, None))
    return jax.shard_map(
        on_device, mesh=mesh, in_specs=in_specs, out_specs=out_specs, check_vma=False
    )
```

time: 77.9 us -> 59.2 us (0.76)
  Pallas kernels: 68.7 us -> 57.1 us
  local copies, waits for them, and re-layouts: 8.24 us -> 1.32 us
    pallas_call x1, Pallas kernels: 68.7 us -> 57.1 us  [on_device(): pl.pallas_call(functools.partial(kernel, dims), out_shape=(vmem((group, s...]
    broadcast_in_dim x4 -> x0, local copies, waits for them, and re-layouts: 5.09 us -> none  [the longest x1 1.28 us: on_device(): layer_scale[None]]
    unnamed x2, local copies, waits for them, and re-layouts: 3.16 us -> 1.32 us
where the time goes in v2:
time: 59.2 us; the launch traced here: 59.1 us
  Pallas kernels  57.1 us (96%)
  local copies, waits for them, and re-layouts  1.32 us (2%)
  between operations  0.64 us (1%)
    pallas_call x1, Pallas kernels, on_device(): pl.pallas_call(functools.partial(kernel, dims), out_shape=(vmem((group, s...  57.1 us
    unnamed x2, local copies, waits for them, and re-layouts  1.32 us

profile of v2, /device:TPU:1, one launch (start us, length us, event | category | flops | bytes accessed | tf_op | source)
XLA Modules:
  0.0 59.1 jit_solution(12572840895670527763)
XLA Ops:
  0.6 57.1 %shard_map.122 = (bf16[192,256]{1,0:T(8,128)(2,1)S(1)}, bf16[128,768]{1,0:T(8,128)(2,1)S(1)}) custom-call(bf16[4,32,768]{2,1,0:T(8,128)(2,1)} %bitcast.13, f32[7,7,768]{2,1,0:T(8,128)} %dwk_h.1, f32[768]{0:T(1024)} %bias_h.1, f32[768]{0:T(1024)} %mixg_h.1, bf16[768,1536]{1,0:T(8,128)(2,1)} %wexp_h.1, bf16[1536,768]{1,0:T(8,128)(2,1)} %wred_h.1, ...), custom_call_target="tpu_custom_call" | custom-call | flops 1811939328 | bytes 8388608 | tf_op jit(solution)/shard_map/pallas_call | solution.py:513
  57.8 0.6 %copy.15 = bf16[1,256,192]{1,2,0:T(8,128)(2,1)} copy(bf16[1,256,192]{1,2,0:T(8,128)(2,1)S(1)} %bitcast.11) | data formatting | bytes 196608
  58.4 0.7 %copy.16 = bf16[1,4,32,768]{3,2,1,0:T(8,128)(2,1)} copy(bf16[1,4,32,768]{3,2,1,0:T(8,128)(2,1)S(1)} %bitcast.10) | data formatting | bytes 393216

commit v3 on v2

--- a/solution.py
+++ b/solution.py
@@ -66,12 +66,12 @@
     sec_h, dwk_h, bias_h, mixg_h, wexp_h, wred_h, scale_h, downg_h, wdt_h, owner_h, gpt_h,
     tok_o, grad_o,
     ext, dwk, bias, mixg, wexp, wred, scale, downg, wdt, owner, gpt,
-    perm, pick, mid_b,
-    sgz, rgz, sgy, rgy, st, rt,
+    perm, pick, middle,
+    sgy, rgy, sgz, rgz, st, rt,
     mixed, normed1, inv1, first, slope, hidden, gpre, proj, normed2, inv2, second,
     gathered, gtok, pair_s, pair_r, own_f, rs_s, rs_r, gfirst, gscaled,
-    load_sem, halo_ss, halo_rs, gz_ss, gz_rs, gy_ss, gy_rs, t_ss, t_rs,
-    ag_ss, ag_rs, fw_ss, fw_rs, pair_ss, pair_rs, rs_ss, rs_rs,
+    load_sem, halo_ss, halo_rs, gy_ss, gy_rs, gz_ss, gz_rs, t_ss, t_rs,
+    ag_ss, ag_rs, fw_ss, fw_rs, pair_ss, pair_rs, rs_ss, rs_rs, known,
 ):
     nz, nx, band, width, chans, hid, group, slots = dims
     n_space = nx * CORES
@@ -97,14 +97,10 @@
 
     barrier = pltpu.get_barrier_semaphore()
 
-    def greet(count, device):
-        @pl.loop(1, count)
-        def _(k):
+    near_z = sorted({k % nz for k in (1, -1, 3, -3, 4, -4)} - {0})
+    for device, away in ((sdev, range(1, n_space)), (ydev, range(1, NY)), (zdev, near_z)):
+        for k in away:
             pl.semaphore_signal(barrier, inc=1, device_id=device(k), device_id_type=MESH)
-
-    greet(n_space, sdev)
-    greet(nz, zdev)
-    greet(NY, ydev)
 
     pairs = [
         (sec_h, ext.at[HALF:HALF + band]), (gpt_h, gpt), (owner_h, owner), (dwk_h, dwk),
@@ -117,10 +113,13 @@
 
     ii = lax.broadcasted_iota(jnp.int32, (slots, slots), 0)
     jj = lax.broadcasted_iota(jnp.int32, (slots, slots), 1)
+    q_z, q_y, q_r = fields(ii, nz, NY, CAP)
+    middle[...] = onehot(jj == q_y * yrows + q_z * CAP + q_r)
     p_y, p_z, p_r = fields(ii, NY, nz, CAP)
-    mid_b[...] = onehot(jj == p_z * zrows + p_y * CAP + p_r)
+    by_y = onehot(jj == p_z * zrows + p_y * CAP + p_r)
+
     loads[1].wait()
-    sgz[...] = dot_nt(onehot(ii == jj), gpt[...]).astype(BF16)
+    sgy[...] = dot_nt(by_y, gpt[...]).astype(BF16)
 
     loads[2].wait()
     named = jnp.broadcast_to(owner[...].astype(F32), (slots, slots))
@@ -130,12 +129,9 @@
     )
     slot = jnp.broadcast_to((owner[...] * CAP).astype(F32) + rank, (slots, slots))
     perm[...] = onehot(ii.astype(F32) == slot)
-    o_z, o_y = fields(owner[...], nz, NY)
-    pos = (o_y * yrows + o_z * CAP).astype(F32) + rank
-    pos = jnp.broadcast_to(pos, (slots, slots))
     u_core, u_x, u_i = fields(ii, CORES, nx, tb)
     pos_col = jnp.sum(
-        jnp.where(jj == (u_x * CORES + u_core) * tb + u_i, pos, 0.0), axis=1, keepdims=True
+        jnp.where(jj == (u_x * CORES + u_core) * tb + u_i, slot, 0.0), axis=1, keepdims=True
     )
     pick[...] = onehot(jj.astype(F32) == pos_col)
 
@@ -149,7 +145,9 @@
     def _():
         ext[HALF + band:] = jnp.zeros((HALF, width, chans), BF16)
 
-    pl.semaphore_wait(barrier, nz + NY + n_space - 3)
+    pl.semaphore_wait(barrier, n_space - 1 + NY - 1 + len(near_z))
+    for k in near_z:
+        pl.semaphore_signal(known, inc=1, device_id=zdev(k), device_id_type=MESH)
 
     def remote(src, dst, ss, rs, device):
         return pltpu.make_async_remote_copy(
@@ -177,35 +175,22 @@
     def block(k_index, size):
         return pl.ds(pl.multiple_of(k_index * size, size), size)
 
+    def far_first(count):
+        return sorted(range(1, count), key=lambda k: -min(k, count - k))
+
     def exchange(src, dst, ss, rs, count, me, size, device):
-        def copy(k):
-            return remote(
-                src.at[block((me + k) % count, size)], dst.at[block(me, size)],
-                ss.at[k], rs.at[k], device(k),
-            )
-
         def begin():
-            @pl.loop(1, count)
-            def _(k):
-                copy(k).start()
-
+            for k in far_first(count):
+                there = block((me + k) % count, size)
+                remote(src.at[there], dst.at[block(me, size)], ss, rs, device(k)).start()
             dst[block(me, size)] = src[block(me, size)]
 
-        def arrive():
-            @pl.loop(1, count)
-            def _(k):
-                copy(k).wait_recv()
-
-        def leave():
-            @pl.loop(1, count)
-            def _(k):
-                copy(k).wait_send()
-
-        return begin, arrive, leave
-
-    gz = exchange(sgz, rgz, gz_ss, gz_rs, nz, z, zrows, zdev)
-    gy = exchange(sgy, rgy, gy_ss, gy_rs, NY, y, yrows, ydev)
-    gz[0]()
+        others = pl.ds(0, (count - 1) * size)
+        return begin, remote(src.at[others], dst.at[others], ss, rs, (dp, partner))
+
+    grads_y, came_y = exchange(sgy, rgy, gy_ss, gy_rs, NY, y, yrows, ydev)
+    grads_z, came_z = exchange(sgz, rgz, gz_ss, gz_rs, nz, z, zrows, zdev)
+    grads_y()
 
     for i in (3, 4, 5):
         loads[i].wait()
@@ -257,7 +242,7 @@
                 r, lanes, HALF, lambda r, i: r + i + band * ((r + i) // HALF)
             )
 
-    @pl.loop(0, band)
+    @pl.loop(0, band, unroll=True)
     def _(r):
         at_rows = block(r, width)
         normed, inv = norm(mixed[at_rows, :])
@@ -267,7 +252,7 @@
 
     loads[6].wait()
 
-    @pl.loop(0, hid // 256)
+    @pl.loop(0, hid // 256, unroll=True)
     def _(j):
         cols = block(j, 256)
         pre = dot(first[...], wexp[:, cols])
@@ -278,7 +263,7 @@
 
     loads[7].wait()
 
-    @pl.loop(0, chans // 256)
+    @pl.loop(0, chans // 256, unroll=True)
     def _(j):
         cols = block(j, 256)
         proj[:, cols] = dot(hidden[...], wred[:, cols])
@@ -286,7 +271,7 @@
     loads[8].wait()
     loads[9].wait()
 
-    @pl.loop(0, band)
+    @pl.loop(0, band, unroll=True)
     def _(r):
         at_rows = block(r, width)
         residual = ext[HALF + r].astype(F32)
@@ -333,9 +318,10 @@
     passed[6].start()
     passed[7].start()
 
-    gz[1]()
-    sgy[...] = dot(mid_b[...], rgz[...]).astype(BF16)
-    gy[0]()
+    pl.semaphore_wait(known, len(near_z))
+    came_y.wait_recv()
+    sgz[...] = dot(middle[...], rgy[...]).astype(BF16)
+    grads_z()
 
     for i in range(4):
         sends[i].wait_recv()
@@ -343,8 +329,8 @@
             sends[4 + i].start()
         passed[i].start()
 
-    gy[1]()
-    gtok[...] = dot(pick[...], rgy[...]).astype(BF16)
+    came_z.wait_recv()
+    gtok[...] = dot(pick[...], rgz[...]).astype(BF16)
     loads[10].wait()
     half = nx * tb
     parts = [slice(q * chans, (q + 1) * chans) for q in range(4)]
@@ -429,17 +415,17 @@
     for c in range(chans // 128):
         gscaled[:, c * 128:(c + 1) * 128] = second[c].astype(BF16)
 
-    @pl.loop(0, hid // 256)
+    @pl.loop(0, hid // 256, unroll=True)
     def _(j):
         cols = block(j, 256)
         gpre[:, cols] = (dot_nt(gscaled[...], wred[cols, :]) * slope[:, cols]).astype(BF16)
 
-    @pl.loop(0, chans // 256)
+    @pl.loop(0, chans // 256, unroll=True)
     def _(j):
         cols = block(j, 256)
         gfirst[:, cols] = dot_nt(gpre[...], wexp[cols, :])
 
-    @pl.loop(0, band)
+    @pl.loop(0, band, unroll=True)
     def _(r):
         at_rows = block(r, width)
         grad = norm_back(gfirst[at_rows, :], normed1[at_rows, :], inv1[at_rows, :], mixg[...])
@@ -465,8 +451,8 @@
     for copy in (*sends, *passed):
         copy.wait_send()
     came.wait_send()
-    for phase in (gz, gy):
-        phase[2]()
+    came_y.wait_send()
+    came_z.wait_send()
 
 
 def on_device(
@@ -503,9 +489,8 @@
         vmem((4, nx * tb, chans), BF16), vmem((4, nx * tb, chans), BF16),
         vmem((rows, chans), F32), vmem((rows, chans), BF16),
         dma((11,)), dma((2,)), dma((2,)),
-        dma((nz,)), dma((nz,)), dma((NY,)), dma((NY,)),
-        dma, dma, dma((6,)), dma((6,)), dma((8,)), dma((8,)), dma((4,)), dma((4,)),
-        dma((4, nx)), dma((4, nx)),
+        dma, dma, dma, dma, dma, dma, dma((6,)), dma((6,)), dma((8,)), dma((8,)), dma((4,)), dma((4,)),
+        dma((4, nx)), dma((4, nx)), pltpu.SemaphoreType.REGULAR,
     ]
     anywhere = pl.BlockSpec(memory_space=pl.ANY)
     inside = pl.BlockSpec(memory_space=pltpu.VMEM)

time: 59.2 us -> 54.8 us (0.926)
  Pallas kernels: 57.1 us -> 52.7 us
    pallas_call x1, Pallas kernels: 57.1 us -> 52.7 us  [on_device(): pl.pallas_call(functools.partial(kernel, dims), out_shape=(vmem((group, s...]
where the time goes in v3:
time: 54.8 us; the launch traced here: 54.6 us
  Pallas kernels  52.7 us (96%)
  local copies, waits for them, and re-layouts  1.32 us (2%)
  between operations  0.64 us (1%)
    pallas_call x1, Pallas kernels, on_device(): pl.pallas_call(functools.partial(kernel, dims), out_shape=(vmem((group, s...  52.7 us
    unnamed x2, local copies, waits for them, and re-layouts  1.32 us

profile of v3, /device:TPU:1, one launch (start us, length us, event | category | flops | bytes accessed | tf_op | source)
XLA Modules:
  0.0 54.6 jit_solution(8106513591150721428)
XLA Ops:
  0.6 52.7 %shard_map.122 = (bf16[192,256]{1,0:T(8,128)(2,1)S(1)}, bf16[128,768]{1,0:T(8,128)(2,1)S(1)}) custom-call(bf16[4,32,768]{2,1,0:T(8,128)(2,1)} %bitcast.13, f32[7,7,768]{2,1,0:T(8,128)} %dwk_h.1, f32[768]{0:T(1024)} %bias_h.1, f32[768]{0:T(1024)} %mixg_h.1, bf16[768,1536]{1,0:T(8,128)(2,1)} %wexp_h.1, bf16[1536,768]{1,0:T(8,128)(2,1)} %wred_h.1, ...), custom_call_target="tpu_custom_call" | custom-call | flops 1811939328 | bytes 8388608 | tf_op jit(solution)/shard_map/pallas_call | solution.py:498
  53.3 0.6 %copy.15 = bf16[1,256,192]{1,2,0:T(8,128)(2,1)} copy(bf16[1,256,192]{1,2,0:T(8,128)(2,1)S(1)} %bitcast.11) | data formatting | bytes 196608
  53.9 0.7 %copy.16 = bf16[1,4,32,768]{3,2,1,0:T(8,128)(2,1)} copy(bf16[1,4,32,768]{3,2,1,0:T(8,128)(2,1)S(1)} %bitcast.10) | data formatting | bytes 393216

commit v4 on v3

--- a/solution.py
+++ b/solution.py
@@ -113,27 +113,11 @@
 
     ii = lax.broadcasted_iota(jnp.int32, (slots, slots), 0)
     jj = lax.broadcasted_iota(jnp.int32, (slots, slots), 1)
-    q_z, q_y, q_r = fields(ii, nz, NY, CAP)
-    middle[...] = onehot(jj == q_y * yrows + q_z * CAP + q_r)
     p_y, p_z, p_r = fields(ii, NY, nz, CAP)
     by_y = onehot(jj == p_z * zrows + p_y * CAP + p_r)
 
     loads[1].wait()
     sgy[...] = dot_nt(by_y, gpt[...]).astype(BF16)
-
-    loads[2].wait()
-    named = jnp.broadcast_to(owner[...].astype(F32), (slots, slots))
-    named_col = jnp.sum(jnp.where(ii == jj, named, 0.0), axis=1, keepdims=True)
-    rank = jnp.sum(
-        jnp.where((named_col == named) & (ii < jj), 1.0, 0.0), axis=0, keepdims=True
-    )
-    slot = jnp.broadcast_to((owner[...] * CAP).astype(F32) + rank, (slots, slots))
-    perm[...] = onehot(ii.astype(F32) == slot)
-    u_core, u_x, u_i = fields(ii, CORES, nx, tb)
-    pos_col = jnp.sum(
-        jnp.where(jj == (u_x * CORES + u_core) * tb + u_i, slot, 0.0), axis=1, keepdims=True
-    )
-    pick[...] = onehot(jj.astype(F32) == pos_col)
 
     loads[0].wait()
 
@@ -223,6 +207,22 @@
             own = convolve(r, lanes, band, lambda r, i: HALF + i)
             mixed[block(r, width), lanes] = own + bias[:, lanes]
 
+    q_z, q_y, q_r = fields(ii, nz, NY, CAP)
+    middle[...] = onehot(jj == q_y * yrows + q_z * CAP + q_r)
+    loads[2].wait()
+    named = jnp.broadcast_to(owner[...].astype(F32), (slots, slots))
+    named_col = jnp.sum(jnp.where(ii == jj, named, 0.0), axis=1, keepdims=True)
+    rank = jnp.sum(
+        jnp.where((named_col == named) & (ii < jj), 1.0, 0.0), axis=0, keepdims=True
+    )
+    slot = jnp.broadcast_to((owner[...] * CAP).astype(F32) + rank, (slots, slots))
+    perm[...] = onehot(ii.astype(F32) == slot)
+    u_core, u_x, u_i = fields(ii, CORES, nx, tb)
+    pos_col = jnp.sum(
+        jnp.where(jj == (u_x * CORES + u_core) * tb + u_i, slot, 0.0), axis=1, keepdims=True
+    )
+    pick[...] = onehot(jj.astype(F32) == pos_col)
+
     @pl.when(sp < n_space - 1)
     def _():
         up.wait_recv()
@@ -235,7 +235,7 @@
     def _(j):
         lanes = block(j, 128)
 
-        @pl.loop(0, band)
+        @pl.loop(0, band, unroll=True)
         def _(r):
             at_rows = block(r, width)
             mixed[at_rows, lanes] += convolve(
@@ -338,11 +338,22 @@
     def pair(q):
         return remote(pair_s.at[q], pair_r.at[q], pair_ss.at[q], pair_rs.at[q], (dp, partner))
 
-    def scatter(q, k):
-        to = pl.ds(k * tb, tb)
+    hb = tb // 2
+
+    def ring(q, i):
+        first_row, target = (
+            (0, right), (hb, left), (tb + hb, right), (tb, left), (2 * tb, right),
+            (2 * tb + hb, left),
+        )[i]
+        at_rows = pl.ds(first_row, hb)
         return remote(
-            rs_s.at[q, to], rs_r.at[q, to], rs_ss.at[q, k], rs_rs.at[q, k], xdev(k)
+            rs_s.at[q, at_rows], rs_r.at[q, at_rows], rs_ss.at[q, i], rs_rs.at[q, i],
+            (dp, target * CORES + core),
         )
+
+    def term(q, chip, h):
+        at_rows = pl.ds(pl.multiple_of(chip * tb + h * hb, hb), hb)
+        return own_f[q, at_rows, :] + pair_r[q, at_rows, :].astype(F32)
 
     for q in range(4):
         pair_s[q] = dot(gtok[block(1 - core, half), :], wdt[:, parts[q]]).astype(BF16)
@@ -355,12 +366,14 @@
     for q in range(4):
         own_f[q] = dot(gtok[block(core, half), :], wdt[:, parts[q]])
         pair(q).wait_recv()
-        for k in (2, 1, 3):
-            there = block((x + k) % nx, tb)
-            rs_s[q, k * tb:(k + 1) * tb, :] = (
-                own_f[q, there, :] + pair_r[q, there, :].astype(F32)
-            ).astype(BF16)
-            scatter(q, k).start()
+        rs_s[q, 0:hb, :] = term(q, over, 0).astype(BF16)
+        ring(q, 0).start()
+        rs_s[q, hb:tb, :] = term(q, over, 1).astype(BF16)
+        ring(q, 1).start()
+        rs_s[q, tb + hb:2 * tb, :] = term(q, right, 1).astype(BF16)
+        ring(q, 2).start()
+        rs_s[q, tb:tb + hb, :] = term(q, left, 0).astype(BF16)
+        ring(q, 3).start()
 
     for copy in passed:
         copy.wait_recv()
@@ -389,15 +402,28 @@
 
     rt[dp] = st[dp]
 
+    for q in range(4):
+        ring(q, 0).wait_recv()
+        rs_s[q, 2 * tb:2 * tb + hb, :] = (
+            term(q, right, 0) + rs_r[q, 0:hb, :].astype(F32)
+        ).astype(BF16)
+        ring(q, 4).start()
+        ring(q, 1).wait_recv()
+        rs_s[q, 2 * tb + hb:3 * tb, :] = (
+            term(q, left, 1) + rs_r[q, hb:tb, :].astype(F32)
+        ).astype(BF16)
+        ring(q, 5).start()
+
     here = block(x, tb)
     gain = downg[...]
     for a in range(2):
         for b in range(2):
             q = 2 * a + b
             grad = own_f[q, here, :] + pair_r[q, here, :].astype(F32)
-            for k in (1, 3, 2):
-                scatter(q, k).wait_recv()
-                grad = grad + rs_r[q, k * tb:(k + 1) * tb, :].astype(F32)
+            for i in range(2, 6):
+                ring(q, i).wait_recv()
+            for slot_at in (tb, 2 * tb):
+                grad = grad + rs_r[q, slot_at:slot_at + tb, :].astype(F32)
             normed = jnp.concatenate([
                 jnp.concatenate(
                     [normed2[c, spots(a, b, big_r), :] for c in range(chans // 128)], axis=1
@@ -446,8 +472,8 @@
 
     for q in range(4):
         pair(q).wait_send()
-        for k in range(1, nx):
-            scatter(q, k).wait_send()
+        for i in range(6):
+            ring(q, i).wait_send()
     for copy in (*sends, *passed):
         copy.wait_send()
     came.wait_send()
@@ -486,11 +512,11 @@
         vmem((n_space * tb, 4 * chans), BF16), vmem((slots, group), BF16),
         vmem((4, nx * tb, chans), BF16), vmem((4, nx * tb, chans), BF16),
         vmem((4, nx * tb, chans), F32),
-        vmem((4, nx * tb, chans), BF16), vmem((4, nx * tb, chans), BF16),
+        vmem((4, 3 * tb, chans), BF16), vmem((4, 3 * tb, chans), BF16),
         vmem((rows, chans), F32), vmem((rows, chans), BF16),
         dma((11,)), dma((2,)), dma((2,)),
         dma, dma, dma, dma, dma, dma, dma((6,)), dma((6,)), dma((8,)), dma((8,)), dma((4,)), dma((4,)),
-        dma((4, nx)), dma((4, nx)), pltpu.SemaphoreType.REGULAR,
+        dma((4, 6)), dma((4, 6)), pltpu.SemaphoreType.REGULAR,
     ]
     anywhere = pl.BlockSpec(memory_space=pl.ANY)
     inside = pl.BlockSpec(memory_space=pltpu.VMEM)

time: 54.8 us -> 53.8 us (0.982)
  Pallas kernels: 52.7 us -> 51.7 us
    pallas_call x1, Pallas kernels: 52.7 us -> 51.7 us  [on_device(): pl.pallas_call(functools.partial(kernel, dims), out_shape=(vmem((group, s...]
where the time goes in v4:
time: 53.8 us; the launch traced here: 53.6 us
  Pallas kernels  51.7 us (96%)
  local copies, waits for them, and re-layouts  1.32 us (2%)
  between operations  0.64 us (1%)
    pallas_call x1, Pallas kernels, on_device(): pl.pallas_call(functools.partial(kernel, dims), out_shape=(vmem((group, s...  51.7 us
    unnamed x2, local copies, waits for them, and re-layouts  1.32 us

profile of v4, /device:TPU:1, one launch (start us, length us, event | category | flops | bytes accessed | tf_op | source)
XLA Modules:
  0.0 53.6 jit_solution(14867147118598326283)
XLA Ops:
  0.6 51.7 %shard_map.122 = (bf16[192,256]{1,0:T(8,128)(2,1)S(1)}, bf16[128,768]{1,0:T(8,128)(2,1)S(1)}) custom-call(bf16[4,32,768]{2,1,0:T(8,128)(2,1)} %bitcast.13, f32[7,7,768]{2,1,0:T(8,128)} %dwk_h.1, f32[768]{0:T(1024)} %bias_h.1, f32[768]{0:T(1024)} %mixg_h.1, bf16[768,1536]{1,0:T(8,128)(2,1)} %wexp_h.1, bf16[1536,768]{1,0:T(8,128)(2,1)} %wred_h.1, ...), custom_call_target="tpu_custom_call" | custom-call | flops 1811939328 | bytes 8388608 | tf_op jit(solution)/shard_map/pallas_call | solution.py:524
  52.3 0.6 %copy.15 = bf16[1,256,192]{1,2,0:T(8,128)(2,1)} copy(bf16[1,256,192]{1,2,0:T(8,128)(2,1)S(1)} %bitcast.11) | data formatting | bytes 196608
  52.9 0.7 %copy.16 = bf16[1,4,32,768]{3,2,1,0:T(8,128)(2,1)} copy(bf16[1,4,32,768]{3,2,1,0:T(8,128)(2,1)S(1)} %bitcast.10) | data formatting | bytes 393216
